TPU v7x, 32 devices: a whole 2x2x4 slice. The times are simulated.
32 devices in a mesh: tm: 16 (over z, y, core), sta: 2 (over x).
Axes of the slice: x: 2, y: 2, z: 4, core: 2. Of those that a mesh axis runs over, the one named last changes fastest.
Arguments:
- data: bfloat16 [64, 3, 6144], P('sta', None, 'tm'), as said below
- bank: bfloat16 [16, 8, 64, 3, 150], P('tm', None, 'sta'), may hold values from -6 to 6
- owners: int32 [2], replicated, may hold values from 0 to 15
- moveouts: int32 [2, 8, 64], P(None, None, 'sta'), may hold values from 0 to 64, as said below
Outputs:
- stack: float32 [2, 8, 6144], P(None, 'sta', 'tm')
Inputs may be any that keep to these rules, and one draw needn't show every extreme that they name: `data`: three-component records with amplitudes that vary from station to station and along time. `moveouts`: delays are relative to the earliest arrival: for each template some station has 0 and some other station has 64.
All inputs are finite; a program needn't handle non-finite values.
Results may differ from a plain program's by a relative error of at most 0.0003.
Values may be sent and summed in bfloat16 or wider, within the bound.
A program may use at most 64 MiB of HBM per device.

v0:
```python
import jax
import jax.numpy as jnp
from jax import lax
from jax.sharding import PartitionSpec as P

MAXM = 64


eps = 1e-06


def passed_along(block, axis, distance):
    devices = range(lax.axis_size(axis))
    route = [(i - distance, i) for i in devices if i - distance in devices]
    return lax.ppermute(block, axis, route)


def correlate(window, batches):
    batch_count, tmpl_count, local_sta, comp_count, span_len = batches.shape
    kernels = jnp.transpose(batches, (2, 0, 1, 3, 4)).reshape(
        local_sta * batch_count * tmpl_count, comp_count, span_len
    )
    records = window.reshape(1, local_sta * comp_count, window.shape[2])
    products = lax.conv_general_dilated(
        records,
        kernels,
        (1,),
        "VALID",
        dimension_numbers=("NCH", "OIH", "NCH"),
        feature_group_count=local_sta,
        preferred_element_type=jnp.float32,
    )
    products = products.reshape(local_sta, batch_count * tmpl_count, products.shape[2])
    squares = jnp.sum(jnp.square(window.astype(jnp.float32)), axis=1)
    energy = lax.reduce_window(squares, 0.0, lax.add, (1, span_len), (1, 1), "VALID") / (
        comp_count * span_len
    )
    tmpl_power = jnp.sum(jnp.square(batches.astype(jnp.float32)), axis=(3, 4)) / (
        comp_count * span_len
    )
    tmpl_power = jnp.transpose(tmpl_power, (2, 0, 1)).reshape(local_sta, batch_count * tmpl_count)
    return products / (
        comp_count
        * span_len
        * jnp.sqrt(tmpl_power + eps)[:, :, None]
        * jnp.sqrt(energy + eps)[None, :, :].transpose(1, 0, 2)
    )


def shift_rows(scores, lag_table, stretch_len):

    def one_row(row, lag_value):
        return lax.dynamic_slice_in_dim(row, lag_value, stretch_len, 0)

    return jax.vmap(jax.vmap(one_row))(scores, lag_table)


def shards(data, bank, owners, moveouts):
    local_sta, comp_count, stretch_len = data.shape
    span_len = bank.shape[-1]
    tmpl_count = bank.shape[1]
    batch_count = owners.shape[0]
    owned_bank = bank[0]
    device_pos = lax.axis_index("tm")
    masked = jnp.stack(
        [
            jnp.where(owners[batch_id] == device_pos, owned_bank.astype(jnp.float32), 0.0)
            for batch_id in range(batch_count)
        ]
    )
    batches = lax.psum(masked, "tm").astype(jnp.bfloat16)
    edge_cells = passed_along(data[:, :, : span_len - 1], "tm", -1)
    scores = correlate(jnp.concatenate([data, edge_cells], axis=2), batches)
    next_scores = passed_along(scores[:, :, :MAXM], "tm", -1)
    scores = jnp.concatenate([scores, next_scores], axis=2)
    lag_table = jnp.transpose(moveouts, (2, 0, 1)).reshape(local_sta, batch_count * tmpl_count)
    shifted = shift_rows(scores, lag_table, stretch_len)
    partial_sum = jnp.sum(shifted, axis=0).reshape(batch_count, tmpl_count, stretch_len)
    return lax.psum_scatter(partial_sum, "sta", scatter_dimension=1, tiled=True)


def solution(mesh):
    placed = (P("sta", None, "tm"), P("tm", None, "sta", None, None), P(), P(None, None, "sta"))
    return jax.shard_map(
        shards, mesh=mesh, in_specs=placed, out_specs=P(None, "sta", "tm"), check_vma=False
    )
```

profile of v0, /device:TPU:0, one launch (start us, length us, event | category | flops | bytes accessed | tf_op | source)
XLA Modules:
  0.0 1866.0 jit_solution(1851045049223399853)
XLA Ops:
  6.3 77.2 %all-reduce.2 = bf16[2,8,32,3,150]{4,1,0,3,2:T(8,128)(2,1)S(1)} all-reduce(f32[2,8,32,3,150]{4,1,0,3,2:T(8,128)S(1)} %pad_maximum_fusion), channel_id=1, replica_groups=mesh['tm'=16,'sta'=2] {'tm'}, use_global_device_ids=true, to_apply=%region_0.1 | all-reduce | flops 230400 | bytes 1382400 | tf_op jit(solution)/shard_map/psum | solution.py:71
  85.3 6.2 copy.35
  91.5 7.8 reduce_window_sum.9
  100.2 12.6 copy.34
  112.8 354.2 %fusion.2 = f32[1,32,16,384]{2,0,1,3:T(1,128)S(1)} fusion(bf16[1,32,3,533]{2,0,1,3:T(2,128)(2,1)} %copy.34, bf16[32,16,3,150]{1,2,0,3:T(4,128)(2,1)} %copy.35), kind=kOutput, calls=%fused_computation.19 | convolution fusion | flops 176947200 | bytes 1349568 | tf_op jit(solution)/shard_map/conv_general_dilated | solution.py:24
  467.1 2.2 multiply_divide_fusion
  469.2 2.7 copy-done
  475.2 5.3 copy.40
  480.6 1376.2 %while.1 = (s32[]{:T(128)}, f32[32,16,448]{2,1,0:T(8,128)S(1)}, s32[512,3]{0,1:T(4,128)S(1)}, f32[512,384]{1,0:T(8,128)S(1)}, s32[]{:T(128)}, /*index=5*/s32[]{:T(128)}) while((s32[]{:T(128)}, f32[32,16,448]{2,1,0:T(8,128)S(1)}, s32[512,3]{0,1:T(4,128)S(1)}, f32[512,384]{1,0:T(8,128)S(1)}, s32[]{:T(128)}, /*index=5*/s32[]{:T(128)}) %tuple.24), condition=%wide.while_cond, body=%wide.while_body.sunk | while | flops 2 | bytes 6289 | solution.py:53
  484.0 2.0 dynamic-slice_bitcast_fusion.2
  486.7 2.0 dynamic-slice_bitcast_fusion.2
  494.7 2.0 dynamic-slice_bitcast_fusion.2
  497.4 2.0 dynamic-slice_bitcast_fusion.2
  502.8 2.0 dynamic-slice_bitcast_fusion.2
  505.5 2.0 dynamic-slice_bitcast_fusion.2
  508.2 2.0 dynamic-slice_bitcast_fusion.2
  513.6 2.0 dynamic-slice_bitcast_fusion.2
  516.2 2.0 dynamic-slice_bitcast_fusion.2
  518.9 2.0 dynamic-slice_bitcast_fusion.2
  524.3 2.0 dynamic-slice_bitcast_fusion.2
  527.0 2.0 dynamic-slice_bitcast_fusion.2
  535.1 2.0 dynamic-slice_bitcast_fusion.2
  537.8 2.0 dynamic-slice_bitcast_fusion.2
  545.8 2.0 dynamic-slice_bitcast_fusion.2
  548.5 2.0 dynamic-slice_bitcast_fusion.2
  553.9 2.0 dynamic-slice_bitcast_fusion.2
  556.6 2.0 dynamic-slice_bitcast_fusion.2
  559.3 2.0 dynamic-slice_bitcast_fusion.2
  564.6 2.0 dynamic-slice_bitcast_fusion.2
  567.3 2.0 dynamic-slice_bitcast_fusion.2
  570.0 2.0 dynamic-slice_bitcast_fusion.2
  1856.9 8.3 all-reduce
  (2069 shorter events, 1332.7 us)
Async XLA Ops:
  0.0 83.9 %copy-start.2 = (bf16[32,3,384]{2,0,1:T(8,128)(2,1)S(1)}, bf16[32,3,384]{2,0,1:T(8,128)(2,1)}, u32[]{:S(2)}) copy-start(bf16[32,3,384]{2,0,1:T(8,128)(2,1)} %param.4) | copy-start | bytes 221188
  0.0 83.9 %copy-start.5 = (s32[2,8,32]{2,1,0:T(8,128)S(1)}, s32[2,8,32]{2,1,0:T(8,128)}, u32[]{:S(2)}) copy-start(s32[2,8,32]{2,1,0:T(8,128)} %param.7) | copy-start | bytes 6148
  0.9 90.6 %collective-permute-start = (bf16[32,3,149]{2,0,1:T(8,128)(2,1)S(1)}, bf16[32,3,149]{2,0,1:T(8,128)(2,1)S(1)}, u32[]{:S(2)}, u32[]{:S(2)}) collective-permute-start(bf16[32,3,149]{2,0,1:T(8,128)(2,1)S(1)} %slice.12), channel_id=1, source_target_pairs={{2,0},{4,2},{6,4},{8,6},{10,8},{12,10},{14,12},{16,14},{18,16},{20... | collective-permute-start | bytes 85832 | tf_op jit(solution)/shard_map/ppermute | solution.py:15
  112.8 354.3 %copy-start.1 = (f32[32,384]{0,1:T(8,128)S(1)}, f32[32,384]{0,1:T(8,128)}, u32[]{:S(2)}) copy-start(f32[32,384]{0,1:T(8,128)} %copy.38) | copy-start | bytes 147460
  112.8 354.3 %copy-start.3 = (f32[32,16]{1,0:T(8,128)S(1)}, f32[32,16]{1,0:T(8,128)}, u32[]{:S(2)}) copy-start(f32[32,16]{1,0:T(8,128)} %copy.37) | copy-start | bytes 6148
  467.0 6.8 copy-start.4
  467.0 7.0 copy-start.6
  469.2 2.7 copy-start
  472.5 8.0 collective-permute-start.1
where the time goes:
time: 1890 us; the launch traced here: 1870 us
  local copies, waits for them, and re-layouts  1400 us (74%)
  matrix products  354 us (19%)
  blocking collectives  85.5 us (5%)
    gather x2048, local copies, waits for them, and re-layouts  1360 us
    conv_general_dilated x1, matrix products, correlate(): lax.conv_general_dilated(records, kernels, (1,), 'VALID', dimension_numbe...  354 us
    psum x1, blocking collectives, shards(): batches = lax.psum(masked, 'tm').astype(jnp.bfloat16)  77.2 us
  transfers between devices with their start and end apart: 2, of which 0 were waited for; matrix products, arithmetic and copies ran while one was open for 1% of the time, Pallas kernels for 0%

commit v1 on v0

v1 whole, which is shorter than its diff:
```python
import functools

import jax
import jax.numpy as jnp
from jax import lax
from jax.experimental import pallas as pl
from jax.experimental.pallas import tpu as pltpu
from jax.sharding import PartitionSpec as P

MAXM = 64
SUB = 16
LANE = 128

eps = 1e-06


def round_up(value, unit):
    return (value + unit - 1) // unit * unit


def window_sums(values, span):
    width = values.shape[-1]

    def ahead(block, distance):
        return pltpu.roll(block, width - distance, axis=1)

    total, done, size, run = None, 0, 1, values
    parts = []
    while size <= span:
        parts.append((size, run))
        if 2 * size <= span:
            run = run + ahead(run, size)
        size *= 2
    for size, run in reversed(parts):
        if done + size <= span:
            piece = run if done == 0 else ahead(run, done)
            total = piece if total is None else total + piece
            done += size
    return total


def spread_kernel(
    blocks, slot_ref, owners_ref, out_ref, sums, core_in, a_near, a_far, b_far, b_near, send, recv
):
    comp_count, local_sta, tmpl_count, span = slot_ref.shape
    depth = round_up(span, SUB)
    lanes = out_ref.shape[2]
    batch_count = owners_ref.shape[0]
    columns = blocks // 4
    me = lax.axis_index("tm")
    core, row, column = me % 2, (me // 2) % 2, me // 4

    def place(at_column, at_row, at_core):
        return (at_column * 2 + at_row) * 2 + at_core

    core_peer = place(column, row, 1 - core)
    row_peer = place(column, 1 - row, core)
    far = [(column + step) % columns for step in range(1, columns)]
    far_peers = [place(other, row, core) for other in far]

    barrier = pltpu.get_barrier_semaphore()
    for peer in [core_peer, row_peer] + far_peers:
        pl.semaphore_signal(
            barrier, inc=1, device_id={"tm": peer}, device_id_type=pl.DeviceIdType.MESH
        )

    lag_at = lax.broadcasted_iota(jnp.int32, (span, lanes), 0)
    slot_at = lax.broadcasted_iota(jnp.int32, (span, lanes), 1)
    taps = jnp.zeros((local_sta * tmpl_count, lanes), jnp.float32)
    for comp in range(comp_count):
        flip = jnp.where(slot_at == (comp + 1) * depth - 1 - lag_at, 1.0, 0.0)
        block = slot_ref[comp].astype(jnp.float32).reshape(local_sta * tmpl_count, span)
        taps = taps + jnp.dot(
            block.astype(jnp.bfloat16),
            flip.astype(jnp.bfloat16),
            preferred_element_type=jnp.float32,
        )
    taps = taps.reshape(local_sta, tmpl_count, lanes)
    sums[...] = jnp.concatenate(
        [jnp.where(owners_ref[batch] == me, taps, 0.0) for batch in range(batch_count)], axis=1
    ).astype(jnp.bfloat16)

    pl.semaphore_wait(barrier, columns + 1)
    used = [0]

    def push(source, target, peer):
        slot = used[0]
        used[0] += 1
        copy = pltpu.make_async_remote_copy(
            src_ref=source,
            dst_ref=target,
            send_sem=send.at[slot],
            recv_sem=recv.at[slot],
            device_id={"tm": peer},
            device_id_type=pl.DeviceIdType.MESH,
        )
        copy.start()
        return copy

    half = local_sta // 2
    part = half // 2
    near, narrow = part // 2, part // columns
    one = near // columns
    base = core * half
    a_base, b_base = base, base + part

    copies = [push(sums.at[pl.ds((1 - core) * half, half)], core_in, core_peer)]
    copies[0].wait()
    mine = pl.ds(base, half)
    sums[mine] = sums[mine] + core_in[...]

    copies = [push(sums.at[pl.ds(a_base + (1 - row) * near, near)], a_near, row_peer)]
    for step in range(columns - 1):
        source = sums.at[pl.ds(b_base + far[step] * narrow, narrow)]
        copies.append(push(source, b_far.at[step], far_peers[step]))
    for copy in copies:
        copy.wait()
    a_mine = a_base + row * near
    b_mine = b_base + column * narrow
    sums[pl.ds(a_mine, near)] = sums[pl.ds(a_mine, near)] + a_near[...]
    total = sums[pl.ds(b_mine, narrow)]
    for step in range(columns - 1):
        total = total + b_far[step]
    sums[pl.ds(b_mine, narrow)] = total

    copies = [push(sums.at[pl.ds(b_mine + (1 - row) * one, one)], b_near, row_peer)]
    for step in range(columns - 1):
        source = sums.at[pl.ds(a_mine + far[step] * one, one)]
        copies.append(push(source, a_far.at[step], far_peers[step]))
    for copy in copies:
        copy.wait()
    a_one = pl.ds(a_mine + column * one, one)
    b_one = pl.ds(b_mine + row * one, one)
    out_ref[b_one] = sums[b_one] + b_near[...]
    total = sums[a_one]
    for step in range(columns - 1):
        total = total + a_far[step]
    out_ref[a_one] = total

    copies = [push(out_ref.at[b_one], out_ref.at[b_one], row_peer)]
    for peer in far_peers:
        copies.append(push(out_ref.at[a_one], out_ref.at[a_one], peer))
    for copy in copies:
        copy.wait()

    a_all, b_all = pl.ds(a_mine, near), pl.ds(b_mine, narrow)
    copies = [push(out_ref.at[a_all], out_ref.at[a_all], row_peer)]
    for peer in far_peers:
        copies.append(push(out_ref.at[b_all], out_ref.at[b_all], peer))
    for copy in copies:
        copy.wait()

    push(out_ref.at[mine], out_ref.at[mine], core_peer).wait()


def spread(slot, owners, blocks):
    comp_count, local_sta, tmpl_count, span = slot.shape
    row_count = owners.shape[0] * tmpl_count
    lanes = round_up(comp_count * round_up(span, SUB), LANE)
    columns = blocks // 4
    part = local_sta // 4
    tile = (row_count, lanes)
    count = 2 + 4 * columns
    return pl.pallas_call(
        functools.partial(spread_kernel, blocks),
        out_shape=jax.ShapeDtypeStruct((local_sta,) + tile, jnp.bfloat16),
        in_specs=[
            pl.BlockSpec(memory_space=pltpu.VMEM),
            pl.BlockSpec(memory_space=pltpu.SMEM),
        ],
        out_specs=pl.BlockSpec(memory_space=pltpu.VMEM),
        scratch_shapes=[
            pltpu.VMEM((local_sta,) + tile, jnp.bfloat16),
            pltpu.VMEM((local_sta // 2,) + tile, jnp.bfloat16),
            pltpu.VMEM((part // 2,) + tile, jnp.bfloat16),
            pltpu.VMEM((columns - 1, part // 2 // columns) + tile, jnp.bfloat16),
            pltpu.VMEM((columns - 1, part // columns) + tile, jnp.bfloat16),
            pltpu.VMEM((part // 2 // columns,) + tile, jnp.bfloat16),
            pltpu.SemaphoreType.DMA((count,)),
            pltpu.SemaphoreType.DMA((count,)),
        ],
        compiler_params=pltpu.CompilerParams(
            collective_id=0, has_side_effects=True, vmem_limit_bytes=32 * 1024 * 1024
        ),
    )(slot, owners)


def spread_by_sum(slot, owners):
    span = slot.shape[3]
    depth = round_up(span, SUB)
    position = lax.axis_index("tm")
    batches = [jnp.where(owners[b] == position, slot, 0) for b in range(owners.shape[0])]
    taps = lax.psum(jnp.concatenate(batches, axis=2), "tm")
    taps = jnp.pad(taps[..., ::-1], ((0, 0), (0, 0), (0, 0), (depth - span, 0)))
    taps = jnp.concatenate(list(taps), axis=2)
    lanes = round_up(taps.shape[2], LANE)
    return jnp.pad(taps, ((0, 0), (0, 0), (0, lanes - taps.shape[2])))


def correlate_kernel(span, stretch, data_ref, taps_ref, lag_ref, out_ref, rows, power):
    local_sta, comp_count, width = data_ref.shape
    _, row_count, lanes = taps_ref.shape
    depth = round_up(span, SUB)
    reach = round_up(stretch + MAXM, LANE)
    scale = 1.0 / (comp_count * span)

    squares = jnp.zeros((local_sta, width), jnp.float32)
    for comp in range(comp_count):
        block = data_ref[:, comp, :].astype(jnp.float32)
        rows[comp] = block
        squares = squares + block * block
    energy = window_sums(squares, span) * scale
    power[...] = (1.0 / jnp.sqrt(energy + eps))[:, :reach]

    def station(index, running):
        pieces = []
        for comp in range(comp_count):
            record = jnp.broadcast_to(rows[comp, pl.ds(index, 1), :], (SUB, width))
            frames = pltpu.roll(record, width - (SUB - 1), axis=1, stride=1, stride_axis=0)
            frames = frames.astype(jnp.bfloat16)
            for start in range(depth - SUB, -1, -SUB):
                moved = frames if start == 0 else pltpu.roll(frames, width - start, axis=1)
                pieces.append(moved[:, :reach])
        while len(pieces) * SUB < lanes:
            pieces.append(jnp.zeros((SUB, reach), jnp.bfloat16))
        taps = taps_ref[index]
        products = jnp.dot(
            taps, jnp.concatenate(pieces, axis=0), preferred_element_type=jnp.float32
        )
        squared = jnp.square(taps.astype(jnp.float32))
        tmpl_power = jnp.sum(squared, axis=1, keepdims=True) * scale
        tmpl_scale = scale / jnp.sqrt(tmpl_power + eps)
        scores = products * power[pl.ds(index, 1), :] * tmpl_scale
        lags = lag_ref[index]
        step = 1
        while step <= MAXM:
            chosen = jnp.broadcast_to((lags & step)[:, :1] != 0, scores.shape)
            scores = jnp.where(chosen, pltpu.roll(scores, reach - step, axis=1), scores)
            step *= 2
        return running + scores[:, :stretch]

    out_ref[...] = lax.fori_loop(
        0, local_sta, station, jnp.zeros((row_count, stretch), jnp.float32), unroll=2
    )


def meet(partial_sum):
    if lax.axis_size("sta") != 2:
        return lax.psum_scatter(partial_sum, "sta", scatter_dimension=1, tiled=True)
    kept = partial_sum.shape[1] // 2
    side = lax.axis_index("sta")
    other = lax.dynamic_slice_in_dim(partial_sum, (1 - side) * kept, kept, 1)
    own = lax.dynamic_slice_in_dim(partial_sum, side * kept, kept, 1)
    return own + lax.ppermute(other, "sta", [(0, 1), (1, 0)])


def shards(data, bank, owners, moveouts):
    local_sta, comp_count, stretch = data.shape
    span = bank.shape[-1]
    tmpl_count = bank.shape[1]
    batch_count = owners.shape[0]
    row_count = batch_count * tmpl_count
    blocks = lax.axis_size("tm")
    edge = span - 1 + MAXM
    width = round_up(stretch + MAXM + round_up(span, SUB), LANE)
    reach = round_up(stretch + MAXM, LANE)

    route = [(i + 1, i) for i in range(blocks - 1)]
    edge_cells = lax.ppermute(data[:, :, :edge], "tm", route)
    slot = jnp.transpose(bank[0], (2, 1, 0, 3))
    if blocks % 4 == 0 and local_sta % (2 * blocks) == 0 and row_count % SUB == 0:
        taps = spread(slot, owners, blocks)
    else:
        taps = spread_by_sum(slot, owners)
    window = jnp.concatenate([data, edge_cells], axis=2)
    window = jnp.pad(window, ((0, 0), (0, 0), (0, width - stretch - edge)))
    lags = jnp.transpose(moveouts, (2, 0, 1)).reshape(local_sta, row_count, 1)
    lags = jnp.broadcast_to(lags, (local_sta, row_count, LANE))

    partial_sum = pl.pallas_call(
        functools.partial(correlate_kernel, span, stretch),
        out_shape=jax.ShapeDtypeStruct((row_count, stretch), jnp.float32),
        in_specs=[pl.BlockSpec(memory_space=pltpu.VMEM)] * 3,
        out_specs=pl.BlockSpec(memory_space=pltpu.VMEM),
        scratch_shapes=[
            pltpu.VMEM((comp_count, local_sta, width), jnp.float32),
            pltpu.VMEM((local_sta, reach), jnp.float32),
        ],
        compiler_params=pltpu.CompilerParams(vmem_limit_bytes=32 * 1024 * 1024),
    )(window, taps, lags)
    return meet(partial_sum.reshape(batch_count, tmpl_count, stretch))


def solution(mesh):
    placed = (P("sta", None, "tm"), P("tm", None, "sta", None, None), P(), P(None, None, "sta"))
    return jax.shard_map(
        shards, mesh=mesh, in_specs=placed, out_specs=P(None, "sta", "tm"), check_vma=False
    )
```

time: 1890 us -> 53 us (0.03); the launches traced: 1870 us -> 52.8 us
  local copies, waits for them, and re-layouts: 1400 us -> 3.05 us
  matrix products: 354 us -> 0 us
  blocking collectives: 85.5 us -> 0 us
  Pallas kernels: 0 us -> 43.9 us
    gather x2049 -> x0, local copies, waits for them, and re-layouts: 1360 us -> none
    conv_general_dilated x1 -> x0, matrix products: 354 us -> none  [correlate(): lax.conv_general_dilated(records, kernels, (1,), 'VALID', dimension_numbe...]
    psum x1 -> x0, blocking collectives: 77.2 us -> none  [shards(): batches = lax.psum(masked, 'tm').astype(jnp.bfloat16)]
    pallas_call x0 -> x2, Pallas kernels: none -> 43.9 us  [the longest x1 26.6 us: spread(): pl.pallas_call(functools.partial(spread_kernel, blocks), out_shape=jax.Sh...]
    reshape x3 -> x0, local copies, waits for them, and re-layouts: 19.5 us -> none  [the longest x1 12.6 us: correlate(): records = window.reshape(1, local_sta * comp_count, window.shape[2])]
  transfers between devices with their start and end apart: 2 -> 2, of which waited for: 0 -> 1; matrix products, arithmetic and copies ran while one was open for 1% -> 2% of each run, Pallas kernels for 0% -> 50%
where the time goes in v1:
time: 53 us; the launch traced here: 52.8 us
  Pallas kernels  43.9 us (83%)
  local copies, waits for them, and re-layouts  3.05 us (6%)
  starting transfers between devices  2.86 us (5%)
  waiting for transfers between devices  2.21 us (4%)
  other arithmetic  0.7 us (1%)
    pallas_call x1, Pallas kernels, spread(): pl.pallas_call(functools.partial(spread_kernel, blocks), out_shape=jax.Sh...  26.6 us
    pallas_call x1, Pallas kernels, shards(): pl.pallas_call(functools.partial(correlate_kernel, span, stretch), out_sh...  17.4 us
    unnamed x6, local copies, waits for them, and re-layouts  2.82 us
    ppermute x1, waiting for transfers between devices, meet(): return own + lax.ppermute(other, 'sta', [(0, 1), (1, 0)])  2.2 us
    ppermute x1, starting transfers between devices, meet(): return own + lax.ppermute(other, 'sta', [(0, 1), (1, 0)])  1.57 us
    ppermute x1, starting transfers between devices, shards(): edge_cells = lax.ppermute(data[:, :, :edge], 'tm', route)  1.29 us
  transfers between devices with their start and end apart: 2, of which 1 were waited for; matrix products, arithmetic and copies ran while one was open for 2% of the time, Pallas kernels for 50%

profile of v1, /device:TPU:0, one launch (start us, length us, event | category | flops | bytes accessed | tf_op | source)
XLA Modules:
  0.0 52.8 jit_solution(6988269243452560233)
XLA Ops:
  0.0 0.9 %copy.6 = bf16[32,3,384]{2,1,0:T(4,128)(2,1)S(1)} copy(bf16[32,3,384]{2,0,1:T(8,128)(2,1)} %param.4) | data formatting | bytes 147456 | tf_op args[0]
  1.0 1.3 %collective-permute-start = (bf16[32,3,213]{2,1,0:T(4,128)(2,1)S(1)}, bf16[32,3,213]{2,1,0:T(4,128)(2,1)S(1)}, u32[]{:S(2)}, u32[]{:S(2)}) collective-permute-start(bf16[32,3,213]{2,1,0:T(4,128)(2,1)S(1)} %slice.4), channel_id=1, source_target_pairs={{2,0},{4,2},{6,4},{8,6},{10,8},{12,10},{14,12},{16,14},{18,16},{20... | collective-permute-start | bytes 122696 | tf_op jit(solution)/shard_map/ppermute | solution.py:269
  2.3 0.0 copy-start.1
  2.3 1.2 %copy.10 = bf16[1,8,32,3,150]{4,1,2,3,0:T(8,128)(2,1)S(1)} copy(bf16[1,8,32,3,150]{4,2,3,1,0:T(8,128)(2,1)} %param.5) | data formatting | bytes 460800 | tf_op args[1]
  3.5 0.0 copy-done.1
  3.5 0.1 copy.8
  3.6 0.0 copy-start
  3.6 0.7 %copy-done = s32[2]{0:T(128)S(1)} copy-done((s32[2]{0:T(128)S(1)}, s32[2]{0:T(128)}, u32[]{:S(2)}) %copy-start) | copy-done | bytes 32
  4.3 26.6 %shard_map.46.taps_ref = bf16[32,16,512]{2,1,0:T(8,128)(2,1)S(1)} custom-call(bf16[3,32,8,150]{3,2,1,0:T(8,128)(2,1)S(1)} %bitcast.9, s32[2]{0:T(128)S(1)} %copy-done), custom_call_target="tpu_custom_call" | custom-call | tf_op jit(solution)/shard_map/pallas_call | solution.py:164
  30.8 0.0 collective-permute-done
  30.8 0.1 fusion.2.data_ref
  30.9 0.1 broadcast_in_dim.8.lag_ref
  31.1 17.4 %shard_map.47 = f32[16,384]{1,0:T(8,128)S(1)} custom-call(bf16[32,3,640]{2,1,0:T(4,128)(2,1)S(1)} %fusion.2.data_ref, bf16[32,16,512]{2,1,0:T(8,128)(2,1)S(1)} %shard_map.46.taps_ref, s32[32,16,128]{2,1,0:T(8,128)S(1)} %broadcast_in_dim.8.lag_ref), custom_call_target="tpu_custom_call" | custom-call | tf_op jit(solution)/shard_map/pallas_call | solution.py:280
  48.5 1.6 %collective-permute-start.1 = (f32[2,4,384]{2,1,0:T(4,128)S(1)}, f32[2,4,384]{2,1,0:T(4,128)S(1)}, u32[]{:S(2)}, u32[]{:S(2)}) collective-permute-start(f32[2,4,384]{2,1,0:T(4,128)S(1)} %constant_dynamic-slice_fusion), channel_id=1, source_target_pairs={{0,1},{1,0},{2,3},{3,2},{4,5},{5,4},{6,7},{7,6},{8,9},{9,8},{10,11... | collective-permute-start | bytes 36872 | tf_op jit(solution)/shard_map/ppermute | solution.py:254
  50.0 2.2 %collective-permute-done.1 = f32[2,4,384]{2,1,0:T(4,128)S(1)} collective-permute-done((f32[2,4,384]{2,1,0:T(4,128)S(1)}, f32[2,4,384]{2,1,0:T(4,128)S(1)}, u32[]{:S(2)}, u32[]{:S(2)}) %collective-permute-start.1) | collective-permute-done | bytes 12320 | tf_op jit(solution)/shard_map/ppermute | solution.py:254
  52.2 0.6 %dynamic-slice_add_fusion = f32[2,4,384]{2,1,0:T(4,128)} fusion(f32[2,4,384]{2,1,0:T(4,128)S(1)} %collective-permute-done.1, f32[2,8,384]{2,1,0:T(8,128)S(1)} %bitcast.11, s32[]{:T(128)S(6)} %select_n.6), kind=kLoop, calls=%fused_computation.5 | loop fusion | flops 3072 | bytes 36868 | tf_op jit(solution)/shard_map/add | solution.py:254
  (2 shorter events, 0.0 us)
Async XLA Ops:
  1.0 29.9 %collective-permute-start = (bf16[32,3,213]{2,1,0:T(4,128)(2,1)S(1)}, bf16[32,3,213]{2,1,0:T(4,128)(2,1)S(1)}, u32[]{:S(2)}, u32[]{:S(2)}) collective-permute-start(bf16[32,3,213]{2,1,0:T(4,128)(2,1)S(1)} %slice.4), channel_id=1, source_target_pairs={{2,0},{4,2},{6,4},{8,6},{10,8},{12,10},{14,12},{16,14},{18,16},{20... | collective-permute-start | bytes 122696 | tf_op jit(solution)/shard_map/ppermute | solution.py:269
  2.3 1.2 %copy-start.1 = (s32[2,8,32]{2,1,0:T(8,128)S(1)}, s32[2,8,32]{2,1,0:T(8,128)}, u32[]{:S(2)}) copy-start(s32[2,8,32]{2,1,0:T(8,128)} %param.7) | copy-start | bytes 6148
  3.6 0.7 %copy-start = (s32[2]{0:T(128)S(1)}, s32[2]{0:T(128)}, u32[]{:S(2)}) copy-start(s32[2]{0:T(128)} %owners_ref.1) | copy-start | bytes 28
  48.5 3.8 %collective-permute-start.1 = (f32[2,4,384]{2,1,0:T(4,128)S(1)}, f32[2,4,384]{2,1,0:T(4,128)S(1)}, u32[]{:S(2)}, u32[]{:S(2)}) collective-permute-start(f32[2,4,384]{2,1,0:T(4,128)S(1)} %constant_dynamic-slice_fusion), channel_id=1, source_target_pairs={{0,1},{1,0},{2,3},{3,2},{4,5},{5,4},{6,7},{7,6},{8,9},{9,8},{10,11... | collective-permute-start | bytes 36872 | tf_op jit(solution)/shard_map/ppermute | solution.py:254

commit v2 on v1

--- a/solution.py
+++ b/solution.py
@@ -39,48 +39,82 @@
     return total
 
 
-def spread_kernel(
-    blocks, slot_ref, owners_ref, out_ref, sums, core_in, a_near, a_far, b_far, b_near, send, recv
+def turned_taps(slot_ref, lanes):
+    tmpl_count, comp_count, local_sta, span = slot_ref.shape
+    depth = round_up(span, SUB)
+    lag_at = lax.broadcasted_iota(jnp.int32, (span, lanes), 0)
+    slot_at = lax.broadcasted_iota(jnp.int32, (span, lanes), 1)
+    taps = jnp.zeros((tmpl_count * local_sta, lanes), jnp.float32)
+    for comp in range(comp_count):
+        flip = jnp.where(slot_at == (comp + 1) * depth - 1 - lag_at, 1.0, 0.0)
+        block = slot_ref[:, comp].reshape(tmpl_count * local_sta, span)
+        taps = taps + jnp.dot(
+            block, flip.astype(jnp.bfloat16), preferred_element_type=jnp.float32
+        )
+    return jnp.swapaxes(taps.reshape(tmpl_count, local_sta, lanes), 0, 1)
+
+
+def network_kernel(
+    blocks,
+    slot_ref,
+    owners_ref,
+    data_ref,
+    moveouts_ref,
+    out_ref,
+    taps,
+    sums,
+    core_in,
+    a_near,
+    a_far,
+    b_far,
+    b_near,
+    edge_in,
+    rows,
+    power,
+    lags,
+    frames,
+    halves,
+    half_in,
+    send,
+    recv,
 ):
-    comp_count, local_sta, tmpl_count, span = slot_ref.shape
+    tmpl_count, comp_count, local_sta, span = slot_ref.shape
+    lanes = taps.shape[2]
+    stretch = data_ref.shape[2]
+    width, reach = rows.shape[2], power.shape[1]
+    batch_count = owners_ref.shape[0]
+    row_count = batch_count * tmpl_count
     depth = round_up(span, SUB)
-    lanes = out_ref.shape[2]
-    batch_count = owners_ref.shape[0]
+    scale = 1.0 / (comp_count * span)
     columns = blocks // 4
     me = lax.axis_index("tm")
+    side = lax.axis_index("sta")
     core, row, column = me % 2, (me // 2) % 2, me // 4
 
     def place(at_column, at_row, at_core):
-        return (at_column * 2 + at_row) * 2 + at_core
+        return {"tm": (at_column * 2 + at_row) * 2 + at_core}
 
     core_peer = place(column, row, 1 - core)
     row_peer = place(column, 1 - row, core)
     far = [(column + step) % columns for step in range(1, columns)]
     far_peers = [place(other, row, core) for other in far]
+    before, after = {"tm": (me + blocks - 1) % blocks}, {"tm": (me + 1) % blocks}
+    sta_peer = {"sta": 1 - side}
 
     barrier = pltpu.get_barrier_semaphore()
-    for peer in [core_peer, row_peer] + far_peers:
+    peers = [core_peer, row_peer, before, after, sta_peer] + far_peers
+    for peer in peers:
         pl.semaphore_signal(
-            barrier, inc=1, device_id={"tm": peer}, device_id_type=pl.DeviceIdType.MESH
-        )
-
-    lag_at = lax.broadcasted_iota(jnp.int32, (span, lanes), 0)
-    slot_at = lax.broadcasted_iota(jnp.int32, (span, lanes), 1)
-    taps = jnp.zeros((local_sta * tmpl_count, lanes), jnp.float32)
-    for comp in range(comp_count):
-        flip = jnp.where(slot_at == (comp + 1) * depth - 1 - lag_at, 1.0, 0.0)
-        block = slot_ref[comp].astype(jnp.float32).reshape(local_sta * tmpl_count, span)
-        taps = taps + jnp.dot(
-            block.astype(jnp.bfloat16),
-            flip.astype(jnp.bfloat16),
-            preferred_element_type=jnp.float32,
-        )
-    taps = taps.reshape(local_sta, tmpl_count, lanes)
+            barrier, inc=1, device_id=peer, device_id_type=pl.DeviceIdType.MESH
+        )
+
+    mine_taps = turned_taps(slot_ref, lanes)
     sums[...] = jnp.concatenate(
-        [jnp.where(owners_ref[batch] == me, taps, 0.0) for batch in range(batch_count)], axis=1
+        [jnp.where(owners_ref[batch] == me, mine_taps, 0.0) for batch in range(batch_count)],
+        axis=1,
     ).astype(jnp.bfloat16)
 
-    pl.semaphore_wait(barrier, columns + 1)
+    pl.semaphore_wait(barrier, len(peers))
     used = [0]
 
     def push(source, target, peer):
@@ -91,11 +125,52 @@
             dst_ref=target,
             send_sem=send.at[slot],
             recv_sem=recv.at[slot],
-            device_id={"tm": peer},
+            device_id=peer,
             device_id_type=pl.DeviceIdType.MESH,
         )
         copy.start()
         return copy
+
+    def build(index, unused):
+        for comp in range(comp_count):
+            record = jnp.broadcast_to(rows[comp, pl.ds(index, 1), :], (SUB, width))
+            record = pltpu.roll(record, width - (SUB - 1), axis=1, stride=1, stride_axis=0)
+            record = record.astype(jnp.bfloat16)
+            moved = {0: record}
+            for place_at in range(depth // SUB):
+                start = depth - SUB - place_at * SUB
+                shift, skip = start % LANE, start // LANE * LANE
+                if shift not in moved:
+                    moved[shift] = pltpu.roll(record, width - shift, axis=1)
+                at = comp * depth + place_at * SUB
+                frames[index, at : at + SUB, :] = moved[shift][:, skip : skip + reach]
+        rest = lanes - comp_count * depth
+        if rest > 0:
+            frames[index, comp_count * depth :, :] = jnp.zeros((rest, reach), jnp.bfloat16)
+        return unused
+
+    def score(index, running):
+        station_taps = taps[index]
+        products = jnp.dot(station_taps, frames[index], preferred_element_type=jnp.float32)
+        squared = jnp.square(station_taps.astype(jnp.float32))
+        tmpl_power = jnp.sum(squared, axis=1, keepdims=True) * scale
+        tmpl_scale = scale / jnp.sqrt(tmpl_power + eps)
+        scores = products * power[pl.ds(index, 1), :] * tmpl_scale
+        delays = lags[index]
+        step = 1
+        while step <= MAXM:
+            chosen = jnp.broadcast_to((delays & step)[:, :1] != 0, scores.shape)
+            scores = jnp.where(chosen, pltpu.roll(scores, reach - step, axis=1), scores)
+            step *= 2
+        return running + scores[:, :stretch]
+
+    def build_some(first, last):
+        lax.fori_loop(first, last, build, 0, unroll=2)
+
+    def score_some(first, count, running):
+        return lax.fori_loop(
+            0, count, lambda i, held: score(first + i, held), running, unroll=min(count, 2)
+        )
 
     half = local_sta // 2
     part = half // 2
@@ -103,16 +178,30 @@
     one = near // columns
     base = core * half
     a_base, b_base = base, base + part
-
+    mine = pl.ds(base, half)
+
+    edge_copy = push(data_ref.at[:, :, pl.ds(0, edge_in.shape[2])], edge_in, before)
     copies = [push(sums.at[pl.ds((1 - core) * half, half)], core_in, core_peer)]
+    delays = moveouts_ref[...]
+    for station in range(local_sta):
+        lags[station] = jnp.broadcast_to(delays[:, station : station + 1], (row_count, LANE))
+    edge_copy.wait()
+    squares = jnp.zeros((local_sta, width), jnp.float32)
+    for comp in range(comp_count):
+        edge = jnp.where(me == blocks - 1, 0.0, edge_in[comp].astype(jnp.float32))
+        block = jnp.concatenate([data_ref[comp].astype(jnp.float32), edge], axis=1)[:, :width]
+        rows[comp] = block
+        squares = squares + block * block
+    energy = window_sums(squares, span) * scale
+    power[...] = (1.0 / jnp.sqrt(energy + eps))[:, :reach]
     copies[0].wait()
-    mine = pl.ds(base, half)
     sums[mine] = sums[mine] + core_in[...]
 
     copies = [push(sums.at[pl.ds(a_base + (1 - row) * near, near)], a_near, row_peer)]
     for step in range(columns - 1):
         source = sums.at[pl.ds(b_base + far[step] * narrow, narrow)]
         copies.append(push(source, b_far.at[step], far_peers[step]))
+    build_some(0, half - 2)
     for copy in copies:
         copy.wait()
     a_mine = a_base + row * near
@@ -127,62 +216,97 @@
     for step in range(columns - 1):
         source = sums.at[pl.ds(a_mine + far[step] * one, one)]
         copies.append(push(source, a_far.at[step], far_peers[step]))
+    build_some(half - 2, half + part)
     for copy in copies:
         copy.wait()
-    a_one = pl.ds(a_mine + column * one, one)
-    b_one = pl.ds(b_mine + row * one, one)
-    out_ref[b_one] = sums[b_one] + b_near[...]
-    total = sums[a_one]
+    a_one, b_one = a_mine + column * one, b_mine + row * one
+    a_two, b_two = pl.ds(a_one, one), pl.ds(b_one, one)
+    taps[b_two] = sums[b_two] + b_near[...]
+    total = sums[a_two]
     for step in range(columns - 1):
         total = total + a_far[step]
-    out_ref[a_one] = total
-
-    copies = [push(out_ref.at[b_one], out_ref.at[b_one], row_peer)]
+    taps[a_two] = total
+
+    copies = [push(taps.at[b_two], taps.at[b_two], row_peer)]
     for peer in far_peers:
-        copies.append(push(out_ref.at[a_one], out_ref.at[a_one], peer))
+        copies.append(push(taps.at[a_two], taps.at[a_two], peer))
+    build_some(half + part, local_sta)
+    running = jnp.zeros((row_count, stretch), jnp.float32)
     for copy in copies:
         copy.wait()
 
     a_all, b_all = pl.ds(a_mine, near), pl.ds(b_mine, narrow)
-    copies = [push(out_ref.at[a_all], out_ref.at[a_all], row_peer)]
+    copies = [push(taps.at[a_all], taps.at[a_all], row_peer)]
     for peer in far_peers:
-        copies.append(push(out_ref.at[b_all], out_ref.at[b_all], peer))
+        copies.append(push(taps.at[b_all], taps.at[b_all], peer))
+    running = score_some(a_mine, near, running)
+    running = score_some(b_mine, narrow, running)
     for copy in copies:
         copy.wait()
 
-    push(out_ref.at[mine], out_ref.at[mine], core_peer).wait()
-
-
-def spread(slot, owners, blocks):
-    comp_count, local_sta, tmpl_count, span = slot.shape
-    row_count = owners.shape[0] * tmpl_count
-    lanes = round_up(comp_count * round_up(span, SUB), LANE)
+    copies = [push(taps.at[mine], taps.at[mine], core_peer)]
+    running = score_some(a_base + (1 - row) * near, near, running)
+    for step in range(columns - 1):
+        running = score_some(b_base + far[step] * narrow, narrow, running)
+    copies[0].wait()
+    running = score_some((1 - core) * half, half, running)
+
+    kept = tmpl_count // 2
+    for which in range(2):
+        halves[which] = jnp.concatenate(
+            [
+                running[batch * tmpl_count + which * kept :][:kept]
+                for batch in range(batch_count)
+            ],
+            axis=0,
+        )
+    copy = push(halves.at[1 - side], half_in, sta_peer)
+    copy.wait()
+    out_ref[...] = halves[side] + half_in[...]
+
+
+def network(slot, owners, data, moveouts, blocks):
+    tmpl_count, comp_count, local_sta, span = slot.shape
+    stretch = data.shape[2]
+    batch_count = owners.shape[0]
+    row_count = batch_count * tmpl_count
+    depth = round_up(span, SUB)
+    lanes = round_up(comp_count * depth, LANE)
+    width = round_up(stretch + MAXM + depth, LANE)
+    reach = round_up(stretch + MAXM, LANE)
     columns = blocks // 4
     part = local_sta // 4
     tile = (row_count, lanes)
-    count = 2 + 4 * columns
+    count = 4 + 4 * columns
+    kept = (row_count // 2, stretch)
+    in_vmem = pl.BlockSpec(memory_space=pltpu.VMEM)
     return pl.pallas_call(
-        functools.partial(spread_kernel, blocks),
-        out_shape=jax.ShapeDtypeStruct((local_sta,) + tile, jnp.bfloat16),
-        in_specs=[
-            pl.BlockSpec(memory_space=pltpu.VMEM),
-            pl.BlockSpec(memory_space=pltpu.SMEM),
-        ],
-        out_specs=pl.BlockSpec(memory_space=pltpu.VMEM),
+        functools.partial(network_kernel, blocks),
+        out_shape=jax.ShapeDtypeStruct(kept, jnp.float32),
+        in_specs=[in_vmem, pl.BlockSpec(memory_space=pltpu.SMEM), in_vmem, in_vmem],
+        out_specs=in_vmem,
         scratch_shapes=[
+            pltpu.VMEM((local_sta,) + tile, jnp.bfloat16),
             pltpu.VMEM((local_sta,) + tile, jnp.bfloat16),
             pltpu.VMEM((local_sta // 2,) + tile, jnp.bfloat16),
             pltpu.VMEM((part // 2,) + tile, jnp.bfloat16),
             pltpu.VMEM((columns - 1, part // 2 // columns) + tile, jnp.bfloat16),
             pltpu.VMEM((columns - 1, part // columns) + tile, jnp.bfloat16),
             pltpu.VMEM((part // 2 // columns,) + tile, jnp.bfloat16),
+            pltpu.VMEM((comp_count, local_sta, width - stretch), jnp.bfloat16),
+            pltpu.VMEM((comp_count, local_sta, width), jnp.float32),
+            pltpu.VMEM((local_sta, reach), jnp.float32),
+            pltpu.VMEM((local_sta, row_count, LANE), jnp.int32),
+            pltpu.VMEM((local_sta, lanes, reach), jnp.bfloat16),
+            pltpu.VMEM((2,) + kept, jnp.float32),
+            pltpu.VMEM(kept, jnp.float32),
             pltpu.SemaphoreType.DMA((count,)),
             pltpu.SemaphoreType.DMA((count,)),
         ],
         compiler_params=pltpu.CompilerParams(
-            collective_id=0, has_side_effects=True, vmem_limit_bytes=32 * 1024 * 1024
+            collective_id=0, has_side_effects=True, vmem_limit_bytes=40 * 1024 * 1024
         ),
-    )(slot, owners)
+    )(slot, owners, data, moveouts)
 
 
 def spread_by_sum(slot, owners):
@@ -244,14 +368,21 @@
     )
 
 
-def meet(partial_sum):
-    if lax.axis_size("sta") != 2:
-        return lax.psum_scatter(partial_sum, "sta", scatter_dimension=1, tiled=True)
-    kept = partial_sum.shape[1] // 2
-    side = lax.axis_index("sta")
-    other = lax.dynamic_slice_in_dim(partial_sum, (1 - side) * kept, kept, 1)
-    own = lax.dynamic_slice_in_dim(partial_sum, side * kept, kept, 1)
-    return own + lax.ppermute(other, "sta", [(0, 1), (1, 0)])
+def fits(data, bank, owners):
+    local_sta, _, stretch = data.shape
+    blocks = lax.axis_size("tm")
+    row_count = owners.shape[0] * bank.shape[1]
+    reach = round_up(bank.shape[-1], SUB) + MAXM
+    return (
+        lax.axis_size("sta") == 2
+        and blocks % 4 == 0
+        and blocks > 4
+        and local_sta % (2 * blocks) == 0
+        and row_count % SUB == 0
+        and bank.shape[1] % 2 == 0
+        and stretch % LANE == 0
+        and stretch >= round_up(reach, LANE)
+    )
 
 
 def shards(data, bank, owners, moveouts):
@@ -261,22 +392,26 @@
     batch_count = owners.shape[0]
     row_count = batch_count * tmpl_count
     blocks = lax.axis_size("tm")
+    if fits(data, bank, owners):
+        kept = network(
+            jnp.transpose(bank[0], (0, 2, 1, 3)),
+            owners,
+            jnp.transpose(data, (1, 0, 2)),
+            moveouts.reshape(row_count, local_sta),
+            blocks,
+        )
+        return kept.reshape(batch_count, tmpl_count // 2, stretch)
+
     edge = span - 1 + MAXM
     width = round_up(stretch + MAXM + round_up(span, SUB), LANE)
     reach = round_up(stretch + MAXM, LANE)
-
     route = [(i + 1, i) for i in range(blocks - 1)]
     edge_cells = lax.ppermute(data[:, :, :edge], "tm", route)
-    slot = jnp.transpose(bank[0], (2, 1, 0, 3))
-    if blocks % 4 == 0 and local_sta % (2 * blocks) == 0 and row_count % SUB == 0:
-        taps = spread(slot, owners, blocks)
-    else:
-        taps = spread_by_sum(slot, owners)
+    taps = spread_by_sum(jnp.transpose(bank[0], (2, 1, 0, 3)), owners)
     window = jnp.concatenate([data, edge_cells], axis=2)
     window = jnp.pad(window, ((0, 0), (0, 0), (0, width - stretch - edge)))
     lags = jnp.transpose(moveouts, (2, 0, 1)).reshape(local_sta, row_count, 1)
     lags = jnp.broadcast_to(lags, (local_sta, row_count, LANE))
-
     partial_sum = pl.pallas_call(
         functools.partial(correlate_kernel, span, stretch),
         out_shape=jax.ShapeDtypeStruct((row_count, stretch), jnp.float32),
@@ -288,7 +423,8 @@
         ],
         compiler_params=pltpu.CompilerParams(vmem_limit_bytes=32 * 1024 * 1024),
     )(window, taps, lags)
-    return meet(partial_sum.reshape(batch_count, tmpl_count, stretch))
+    partial_sum = partial_sum.reshape(batch_count, tmpl_count, stretch)
+    return lax.psum_scatter(partial_sum, "sta", scatter_dimension=1, tiled=True)
 
 
 def solution(mesh):

time: 53 us -> 41.4 us (0.78)
  Pallas kernels: 43.9 us -> 37.3 us
  starting transfers between devices: 2.86 us -> 0 us
  waiting for transfers between devices: 2.21 us -> 0 us
  local copies, waits for them, and re-layouts: 3.05 us -> 3.84 us
  other arithmetic: 0.7 us -> 0 us
    pallas_call x2 -> x1, Pallas kernels: 43.9 us -> 37.3 us  [network(): pl.pallas_call(functools.partial(network_kernel, blocks), out_shape=jax.S...]
    ppermute x2 -> x0, starting transfers between devices: 2.86 us -> none  [the longest x1 1.57 us: meet(): return own + lax.ppermute(other, 'sta', [(0, 1), (1, 0)])]
    ppermute x2 -> x0, waiting for transfers between devices: 2.21 us -> none  [the longest x1 2.2 us: meet(): return own + lax.ppermute(other, 'sta', [(0, 1), (1, 0)])]
    reshape x0 -> x1, local copies, waits for them, and re-layouts: none -> 0.61 us  [shards(): return kept.reshape(batch_count, tmpl_count // 2, stretch)]
    add x1 -> x0, other arithmetic: 0.61 us -> none  [meet(): return own + lax.ppermute(other, 'sta', [(0, 1), (1, 0)])]
    unnamed x6 -> x8, local copies, waits for them, and re-layouts: 2.82 us -> 3.23 us
  transfers between devices with their start and end apart: 2 -> 0, of which waited for: 1 -> 0; matrix products, arithmetic and copies ran while one was open for 2% -> 0% of each run, Pallas kernels for 50% -> 0%
where the time goes in v2:
time: 41.4 us; the launch traced here: 41.1 us
  Pallas kernels  37.3 us (90%)
  local copies, waits for them, and re-layouts  3.84 us (9%)
    pallas_call x1, Pallas kernels, network(): pl.pallas_call(functools.partial(network_kernel, blocks), out_shape=jax.S...  37.3 us
    unnamed x8, local copies, waits for them, and re-layouts  3.23 us

profile of v2, /device:TPU:0, one launch (start us, length us, event | category | flops | bytes accessed | tf_op | source)
XLA Modules:
  0.0 41.1 jit_solution(10687222721373926419)
XLA Ops:
  0.0 0.0 copy-start.3
  0.0 0.7 %copy-done.3 = s32[2]{0:T(128)S(1)} copy-done((s32[2]{0:T(128)S(1)}, s32[2]{0:T(128)}, u32[]{:S(2)}) %copy-start.3) | copy-done | bytes 32
  0.7 0.0 copy-start
  0.7 1.0 %copy-done = bf16[1,8,32,3,150]{4,2,3,1,0:T(8,128)(2,1)S(1)} copy-done((bf16[1,8,32,3,150]{4,2,3,1,0:T(8,128)(2,1)S(1)}, bf16[1,8,32,3,150]{4,2,3,1,0:T(8,128)(2,1)}, u32[]{:S(2)}) %copy-start) | copy-done | bytes 230424
  1.7 0.0 copy-start.1
  1.7 0.9 %copy-done.1 = bf16[32,3,384]{2,0,1:T(8,128)(2,1)S(1)} copy-done((bf16[32,3,384]{2,0,1:T(8,128)(2,1)S(1)}, bf16[32,3,384]{2,0,1:T(8,128)(2,1)}, u32[]{:S(2)}) %copy-start.1) | copy-done | bytes 73752
  2.5 0.0 copy-start.2
  2.5 0.7 %copy-done.2 = s32[2,8,32]{2,1,0:T(8,128)S(1)} copy-done((s32[2,8,32]{2,1,0:T(8,128)S(1)}, s32[2,8,32]{2,1,0:T(8,128)}, u32[]{:S(2)}) %copy-start.2) | copy-done | bytes 2072
  3.2 37.3 %shard_map.46 = f32[8,384]{1,0:T(8,128)S(1)} custom-call(bf16[8,3,32,150]{3,2,1,0:T(8,128)(2,1)S(1)} %bitcast.5, s32[2]{0:T(128)S(1)} %copy-done.3, bf16[3,32,384]{2,1,0:T(8,128)(2,1)S(1)} %bitcast.6, s32[16,32]{1,0:T(8,128)S(1)} %bitcast.7), custom_call_target="tpu_custom_call" | custom-call | tf_op jit(solution)/shard_map/pallas_call | solution.py:283
  40.5 0.6 %reshape.7 = f32[2,4,384]{2,1,0:T(4,128)} reshape(f32[8,384]{1,0:T(8,128)S(1)} %shard_map.46) | data formatting | bytes 24576 | tf_op jit(solution)/shard_map/reshape | solution.py:403
Async XLA Ops:
  0.0 0.7 %copy-start.3 = (s32[2]{0:T(128)S(1)}, s32[2]{0:T(128)}, u32[]{:S(2)}) copy-start(s32[2]{0:T(128)} %owners_ref.1) | copy-start | bytes 28
  0.7 1.0 %copy-start = (bf16[1,8,32,3,150]{4,2,3,1,0:T(8,128)(2,1)S(1)}, bf16[1,8,32,3,150]{4,2,3,1,0:T(8,128)(2,1)}, u32[]{:S(2)}) copy-start(bf16[1,8,32,3,150]{4,2,3,1,0:T(8,128)(2,1)} %param.5) | copy-start | bytes 691204
  1.7 0.9 %copy-start.1 = (bf16[32,3,384]{2,0,1:T(8,128)(2,1)S(1)}, bf16[32,3,384]{2,0,1:T(8,128)(2,1)}, u32[]{:S(2)}) copy-start(bf16[32,3,384]{2,0,1:T(8,128)(2,1)} %param.4) | copy-start | bytes 221188
  2.5 0.7 %copy-start.2 = (s32[2,8,32]{2,1,0:T(8,128)S(1)}, s32[2,8,32]{2,1,0:T(8,128)}, u32[]{:S(2)}) copy-start(s32[2,8,32]{2,1,0:T(8,128)} %param.7) | copy-start | bytes 6148

commit v3 on v2

--- a/solution.py
+++ b/solution.py
@@ -10,6 +10,7 @@
 MAXM = 64
 SUB = 16
 LANE = 128
+PHASES = 4
 
 eps = 1e-06
 
@@ -39,28 +40,59 @@
     return total
 
 
-def turned_taps(slot_ref, lanes):
+def laid_taps(slot_ref, lanes):
     tmpl_count, comp_count, local_sta, span = slot_ref.shape
     depth = round_up(span, SUB)
     lag_at = lax.broadcasted_iota(jnp.int32, (span, lanes), 0)
     slot_at = lax.broadcasted_iota(jnp.int32, (span, lanes), 1)
     taps = jnp.zeros((tmpl_count * local_sta, lanes), jnp.float32)
     for comp in range(comp_count):
-        flip = jnp.where(slot_at == (comp + 1) * depth - 1 - lag_at, 1.0, 0.0)
+        laid = jnp.where(slot_at == comp * depth + lag_at, 1.0, 0.0)
         block = slot_ref[:, comp].reshape(tmpl_count * local_sta, span)
         taps = taps + jnp.dot(
-            block, flip.astype(jnp.bfloat16), preferred_element_type=jnp.float32
+            block, laid.astype(jnp.bfloat16), preferred_element_type=jnp.float32
         )
     return jnp.swapaxes(taps.reshape(tmpl_count, local_sta, lanes), 0, 1)
+
+
+def ahead(block, distance):
+    width = block.shape[-1]
+    return block if distance == 0 else pltpu.roll(block, width - distance, axis=block.ndim - 1)
+
+
+def phase_energies(squares, span):
+    inner_last = span // PHASES
+    groups = sum(squares[1:], squares[0])
+    inner, size, done, run = None, 1, 1, groups
+    length = inner_last - 1
+    while size <= length:
+        if length & size:
+            piece = ahead(run, done)
+            inner = piece if inner is None else inner + piece
+            done += size
+        run = run + ahead(run, size)
+        size *= 2
+    energies = []
+    for phase in range(PHASES):
+        total = inner
+        for step in range(phase, phase + span):
+            at, which = step // PHASES, step % PHASES
+            if not 1 <= at < inner_last:
+                total = total + ahead(squares[which], at)
+        energies.append(total)
+    return energies
 
 
 def network_kernel(
     blocks,
+    slot_hbm,
+    owners_ref,
+    data_hbm,
+    moveouts_hbm,
+    out_ref,
     slot_ref,
-    owners_ref,
     data_ref,
     moveouts_ref,
-    out_ref,
     taps,
     sums,
     core_in,
@@ -75,13 +107,21 @@
     frames,
     halves,
     half_in,
+    local,
     send,
     recv,
 ):
+    loads = [
+        pltpu.make_async_copy(slot_hbm, slot_ref, local.at[0]),
+        pltpu.make_async_copy(data_hbm, data_ref, local.at[1]),
+        pltpu.make_async_copy(moveouts_hbm, moveouts_ref, local.at[2]),
+    ]
+    for load in loads:
+        load.start()
     tmpl_count, comp_count, local_sta, span = slot_ref.shape
     lanes = taps.shape[2]
     stretch = data_ref.shape[2]
-    width, reach = rows.shape[2], power.shape[1]
+    width = stretch + edge_in.shape[2]
     batch_count = owners_ref.shape[0]
     row_count = batch_count * tmpl_count
     depth = round_up(span, SUB)
@@ -108,7 +148,8 @@
             barrier, inc=1, device_id=peer, device_id_type=pl.DeviceIdType.MESH
         )
 
-    mine_taps = turned_taps(slot_ref, lanes)
+    loads[0].wait()
+    mine_taps = laid_taps(slot_ref, lanes)
     sums[...] = jnp.concatenate(
         [jnp.where(owners_ref[batch] == me, mine_taps, 0.0) for batch in range(batch_count)],
         axis=1,
@@ -132,37 +173,54 @@
         return copy
 
     def build(index, unused):
+        upper = lax.broadcasted_iota(jnp.int32, (2 * PHASES, 2 * LANE), 0) < PHASES
         for comp in range(comp_count):
-            record = jnp.broadcast_to(rows[comp, pl.ds(index, 1), :], (SUB, width))
-            record = pltpu.roll(record, width - (SUB - 1), axis=1, stride=1, stride_axis=0)
-            record = record.astype(jnp.bfloat16)
-            moved = {0: record}
-            for place_at in range(depth // SUB):
-                start = depth - SUB - place_at * SUB
-                shift, skip = start % LANE, start // LANE * LANE
-                if shift not in moved:
-                    moved[shift] = pltpu.roll(record, width - shift, axis=1)
-                at = comp * depth + place_at * SUB
-                frames[index, at : at + SUB, :] = moved[shift][:, skip : skip + reach]
+            record = rows[comp * local_sta + index]
+            groups = []
+            for pair in range(SUB // (2 * PHASES)):
+                groups.append(
+                    jnp.where(upper, ahead(record, 2 * pair), ahead(record, 2 * pair + 1))
+                )
+            record = jnp.concatenate(groups, axis=0).astype(jnp.bfloat16)
+            for group in range(depth // SUB):
+                at = comp * depth + group * SUB
+                frames[index, at : at + SUB, :] = ahead(record, group * SUB // PHASES)[:, :LANE]
         rest = lanes - comp_count * depth
         if rest > 0:
-            frames[index, comp_count * depth :, :] = jnp.zeros((rest, reach), jnp.bfloat16)
+            frames[index, comp_count * depth :, :] = jnp.zeros((rest, LANE), jnp.bfloat16)
         return unused
 
     def score(index, running):
         station_taps = taps[index]
-        products = jnp.dot(station_taps, frames[index], preferred_element_type=jnp.float32)
+        moved = [station_taps]
+        for phase in range(1, PHASES):
+            moved.append(pltpu.roll(station_taps, phase, axis=1))
+        products = jnp.dot(
+            jnp.concatenate(moved, axis=0), frames[index], preferred_element_type=jnp.float32
+        )
         squared = jnp.square(station_taps.astype(jnp.float32))
         tmpl_power = jnp.sum(squared, axis=1, keepdims=True) * scale
         tmpl_scale = scale / jnp.sqrt(tmpl_power + eps)
-        scores = products * power[pl.ds(index, 1), :] * tmpl_scale
+        scores = [
+            products[phase * row_count : (phase + 1) * row_count]
+            * power[phase, pl.ds(index, 1), :]
+            * tmpl_scale
+            for phase in range(PHASES)
+        ]
         delays = lags[index]
         step = 1
         while step <= MAXM:
-            chosen = jnp.broadcast_to((delays & step)[:, :1] != 0, scores.shape)
-            scores = jnp.where(chosen, pltpu.roll(scores, reach - step, axis=1), scores)
+            chosen = (delays & step) != 0
+            scores = [
+                jnp.where(
+                    chosen,
+                    ahead(scores[(phase + step) % PHASES], (phase + step) // PHASES),
+                    scores[phase],
+                )
+                for phase in range(PHASES)
+            ]
             step *= 2
-        return running + scores[:, :stretch]
+        return tuple(held + score for held, score in zip(running, scores))
 
     def build_some(first, last):
         lax.fori_loop(first, last, build, 0, unroll=2)
@@ -180,20 +238,37 @@
     a_base, b_base = base, base + part
     mine = pl.ds(base, half)
 
+    loads[1].wait()
     edge_copy = push(data_ref.at[:, :, pl.ds(0, edge_in.shape[2])], edge_in, before)
     copies = [push(sums.at[pl.ds((1 - core) * half, half)], core_in, core_peer)]
+    loads[2].wait()
     delays = moveouts_ref[...]
     for station in range(local_sta):
         lags[station] = jnp.broadcast_to(delays[:, station : station + 1], (row_count, LANE))
     edge_copy.wait()
-    squares = jnp.zeros((local_sta, width), jnp.float32)
+    pieces = []
     for comp in range(comp_count):
         edge = jnp.where(me == blocks - 1, 0.0, edge_in[comp].astype(jnp.float32))
-        block = jnp.concatenate([data_ref[comp].astype(jnp.float32), edge], axis=1)[:, :width]
-        rows[comp] = block
-        squares = squares + block * block
-    energy = window_sums(squares, span) * scale
-    power[...] = (1.0 / jnp.sqrt(energy + eps))[:, :reach]
+        pieces.append(jnp.concatenate([data_ref[comp].astype(jnp.float32), edge], axis=1))
+    window = jnp.concatenate(pieces, axis=0)
+    time_at = lax.broadcasted_iota(jnp.int32, (width, 2 * LANE), 0)
+    slot_at = lax.broadcasted_iota(jnp.int32, (width, 2 * LANE), 1)
+    picked = jnp.where(time_at == PHASES * slot_at, 1.0, 0.0).astype(jnp.bfloat16)
+    phased, squares = [], []
+    for phase in range(PHASES):
+        found = jnp.dot(
+            ahead(window, phase).astype(jnp.bfloat16), picked, preferred_element_type=jnp.float32
+        )
+        phased.append(found)
+        squares.append(
+            sum(
+                jnp.square(found[comp * local_sta : (comp + 1) * local_sta])
+                for comp in range(comp_count)
+            )
+        )
+    rows[...] = jnp.swapaxes(jnp.stack(phased + phased, axis=0), 0, 1)
+    for phase, energy in enumerate(phase_energies(squares, span)):
+        power[phase] = (1.0 / jnp.sqrt(energy * scale + eps))[:, :LANE]
     copies[0].wait()
     sums[mine] = sums[mine] + core_in[...]
 
@@ -201,7 +276,7 @@
     for step in range(columns - 1):
         source = sums.at[pl.ds(b_base + far[step] * narrow, narrow)]
         copies.append(push(source, b_far.at[step], far_peers[step]))
-    build_some(0, half - 2)
+    build_some(0, half)
     for copy in copies:
         copy.wait()
     a_mine = a_base + row * near
@@ -216,7 +291,7 @@
     for step in range(columns - 1):
         source = sums.at[pl.ds(a_mine + far[step] * one, one)]
         copies.append(push(source, a_far.at[step], far_peers[step]))
-    build_some(half - 2, half + part)
+    build_some(half, half + part + near)
     for copy in copies:
         copy.wait()
     a_one, b_one = a_mine + column * one, b_mine + row * one
@@ -230,8 +305,8 @@
     copies = [push(taps.at[b_two], taps.at[b_two], row_peer)]
     for peer in far_peers:
         copies.append(push(taps.at[a_two], taps.at[a_two], peer))
-    build_some(half + part, local_sta)
-    running = jnp.zeros((row_count, stretch), jnp.float32)
+    build_some(half + part + near, local_sta)
+    running = (jnp.zeros((row_count, LANE), jnp.float32),) * PHASES
     for copy in copies:
         copy.wait()
 
@@ -255,14 +330,28 @@
     for which in range(2):
         halves[which] = jnp.concatenate(
             [
-                running[batch * tmpl_count + which * kept :][:kept]
+                held[batch * tmpl_count + which * kept :][:kept]
+                for held in running
                 for batch in range(batch_count)
             ],
             axis=0,
         )
     copy = push(halves.at[1 - side], half_in, sta_peer)
+    slot_at = lax.broadcasted_iota(jnp.int32, (LANE, stretch), 0)
+    time_at = lax.broadcasted_iota(jnp.int32, (LANE, stretch), 1)
     copy.wait()
-    out_ref[...] = halves[side] + half_in[...]
+    summed = halves[side] + half_in[...]
+    kept_rows = batch_count * kept
+    result = jnp.zeros((kept_rows, stretch), jnp.float32)
+    for phase in range(PHASES):
+        placed = jnp.where(time_at == PHASES * slot_at + phase, 1.0, 0.0)
+        result = result + jnp.dot(
+            summed[phase * kept_rows : (phase + 1) * kept_rows],
+            placed,
+            precision=lax.Precision.HIGHEST,
+            preferred_element_type=jnp.float32,
+        )
+    out_ref[...] = result
 
 
 def network(slot, owners, data, moveouts, blocks):
@@ -273,19 +362,23 @@
     depth = round_up(span, SUB)
     lanes = round_up(comp_count * depth, LANE)
     width = round_up(stretch + MAXM + depth, LANE)
-    reach = round_up(stretch + MAXM, LANE)
     columns = blocks // 4
     part = local_sta // 4
     tile = (row_count, lanes)
     count = 4 + 4 * columns
     kept = (row_count // 2, stretch)
+    phased = (PHASES * row_count // 2, LANE)
+    anywhere = pl.BlockSpec(memory_space=pl.ANY)
     in_vmem = pl.BlockSpec(memory_space=pltpu.VMEM)
     return pl.pallas_call(
         functools.partial(network_kernel, blocks),
         out_shape=jax.ShapeDtypeStruct(kept, jnp.float32),
-        in_specs=[in_vmem, pl.BlockSpec(memory_space=pltpu.SMEM), in_vmem, in_vmem],
+        in_specs=[anywhere, pl.BlockSpec(memory_space=pltpu.SMEM), anywhere, anywhere],
         out_specs=in_vmem,
         scratch_shapes=[
+            pltpu.VMEM(slot.shape, slot.dtype),
+            pltpu.VMEM(data.shape, data.dtype),
+            pltpu.VMEM(moveouts.shape, moveouts.dtype),
             pltpu.VMEM((local_sta,) + tile, jnp.bfloat16),
             pltpu.VMEM((local_sta,) + tile, jnp.bfloat16),
             pltpu.VMEM((local_sta // 2,) + tile, jnp.bfloat16),
@@ -294,17 +387,18 @@
             pltpu.VMEM((columns - 1, part // columns) + tile, jnp.bfloat16),
             pltpu.VMEM((part // 2 // columns,) + tile, jnp.bfloat16),
             pltpu.VMEM((comp_count, local_sta, width - stretch), jnp.bfloat16),
-            pltpu.VMEM((comp_count, local_sta, width), jnp.float32),
-            pltpu.VMEM((local_sta, reach), jnp.float32),
+            pltpu.VMEM((comp_count * local_sta, 2 * PHASES, 2 * LANE), jnp.float32),
+            pltpu.VMEM((PHASES, local_sta, LANE), jnp.float32),
             pltpu.VMEM((local_sta, row_count, LANE), jnp.int32),
-            pltpu.VMEM((local_sta, lanes, reach), jnp.bfloat16),
-            pltpu.VMEM((2,) + kept, jnp.float32),
-            pltpu.VMEM(kept, jnp.float32),
+            pltpu.VMEM((local_sta, lanes, LANE), jnp.bfloat16),
+            pltpu.VMEM((2,) + phased, jnp.float32),
+            pltpu.VMEM(phased, jnp.float32),
+            pltpu.SemaphoreType.DMA((3,)),
             pltpu.SemaphoreType.DMA((count,)),
             pltpu.SemaphoreType.DMA((count,)),
         ],
         compiler_params=pltpu.CompilerParams(
-            collective_id=0, has_side_effects=True, vmem_limit_bytes=40 * 1024 * 1024
+            collective_id=0, has_side_effects=True, vmem_limit_bytes=60 * 1024 * 1024
         ),
     )(slot, owners, data, moveouts)
 
@@ -382,6 +476,10 @@
         and bank.shape[1] % 2 == 0
         and stretch % LANE == 0
         and stretch >= round_up(reach, LANE)
+        and stretch + MAXM <= PHASES * LANE
+        and bank.shape[1] // 2 * owners.shape[0] % 8 == 0
+        and bank.shape[-1] >= 4 * PHASES
+        and reach - MAXM <= PHASES * LANE
     )
 
 

time: 41.4 us -> 39 us (0.942)
  local copies, waits for them, and re-layouts: 3.84 us -> 1.31 us
    unnamed x8 -> x0, local copies, waits for them, and re-layouts: 3.23 us -> none
    reshape x1, local copies, waits for them, and re-layouts: 0.61 us -> 1.31 us  [shards(): return kept.reshape(batch_count, tmpl_count // 2, stretch)]
where the time goes in v3:
time: 39 us; the launch traced here: 38.8 us
  Pallas kernels  37.5 us (96%)
  local copies, waits for them, and re-layouts  1.31 us (3%)
    pallas_call x1, Pallas kernels, network(): pl.pallas_call(functools.partial(network_kernel, blocks), out_shape=jax.S...  37.5 us
    reshape x1, local copies, waits for them, and re-layouts, shards(): return kept.reshape(batch_count, tmpl_count // 2, stretch)  1.31 us

profile of v3, /device:TPU:0, one launch (start us, length us, event | category | flops | bytes accessed | tf_op | source)
XLA Modules:
  0.0 38.8 jit_solution(15824512740039896865)
XLA Ops:
  0.0 37.5 %shard_map.46 = f32[8,384]{1,0:T(8,128)} custom-call(bf16[8,3,32,150]{3,2,1,0:T(8,128)(2,1)} %bitcast.5, s32[2]{0:T(128)} %owners_ref.1, bf16[3,32,384]{2,1,0:T(8,128)(2,1)} %bitcast.6, s32[16,32]{1,0:T(8,128)} %bitcast.7), custom_call_target="tpu_custom_call" | custom-call | tf_op jit(solution)/shard_map/pallas_call | solution.py:373
  37.5 1.3 %reshape.7 = f32[2,4,384]{2,1,0:T(4,128)} reshape(f32[8,384]{1,0:T(8,128)} %shard_map.46) | data formatting | bytes 24576 | tf_op jit(solution)/shard_map/reshape | solution.py:501

commit v4 on v3

--- a/solution.py
+++ b/solution.py
@@ -94,12 +94,8 @@
     data_ref,
     moveouts_ref,
     taps,
-    sums,
-    core_in,
-    a_near,
-    a_far,
-    b_far,
-    b_near,
+    parcels,
+    inbox,
     edge_in,
     rows,
     power,
@@ -138,11 +134,11 @@
     row_peer = place(column, 1 - row, core)
     far = [(column + step) % columns for step in range(1, columns)]
     far_peers = [place(other, row, core) for other in far]
-    before, after = {"tm": (me + blocks - 1) % blocks}, {"tm": (me + 1) % blocks}
+    others = [(me + step) % blocks for step in range(1, blocks)]
     sta_peer = {"sta": 1 - side}
 
     barrier = pltpu.get_barrier_semaphore()
-    peers = [core_peer, row_peer, before, after, sta_peer] + far_peers
+    peers = [sta_peer] + [{"tm": other} for other in others]
     for peer in peers:
         pl.semaphore_signal(
             barrier, inc=1, device_id=peer, device_id_type=pl.DeviceIdType.MESH
@@ -150,10 +146,16 @@
 
     loads[0].wait()
     mine_taps = laid_taps(slot_ref, lanes)
-    sums[...] = jnp.concatenate(
-        [jnp.where(owners_ref[batch] == me, mine_taps, 0.0) for batch in range(batch_count)],
-        axis=1,
-    ).astype(jnp.bfloat16)
+    half = local_sta // 2
+    part = half // 2
+    near, narrow = part // 2, part // columns
+    for other in range(blocks):
+        at_core, at_row, at_column = other % 2, (other // 2) % 2, other // 4
+        a_at = at_core * half + at_row * near + at_column
+        b_at = at_core * half + part + at_column * narrow + at_row
+        parcels[other] = jnp.concatenate([mine_taps[a_at], mine_taps[b_at]], axis=0).astype(
+            jnp.bfloat16
+        )
 
     pl.semaphore_wait(barrier, len(peers))
     used = [0]
@@ -230,17 +232,13 @@
             0, count, lambda i, held: score(first + i, held), running, unroll=min(count, 2)
         )
 
-    half = local_sta // 2
-    part = half // 2
-    near, narrow = part // 2, part // columns
-    one = near // columns
     base = core * half
     a_base, b_base = base, base + part
     mine = pl.ds(base, half)
 
+    copies = [push(parcels.at[other], inbox.at[me], {"tm": other}) for other in others]
     loads[1].wait()
-    edge_copy = push(data_ref.at[:, :, pl.ds(0, edge_in.shape[2])], edge_in, before)
-    copies = [push(sums.at[pl.ds((1 - core) * half, half)], core_in, core_peer)]
+    edge_copy = push(data_ref.at[:, :, pl.ds(0, edge_in.shape[2])], edge_in, {"tm": others[-1]})
     loads[2].wait()
     delays = moveouts_ref[...]
     for station in range(local_sta):
@@ -269,38 +267,19 @@
     rows[...] = jnp.swapaxes(jnp.stack(phased + phased, axis=0), 0, 1)
     for phase, energy in enumerate(phase_energies(squares, span)):
         power[phase] = (1.0 / jnp.sqrt(energy * scale + eps))[:, :LANE]
-    copies[0].wait()
-    sums[mine] = sums[mine] + core_in[...]
-
-    copies = [push(sums.at[pl.ds(a_base + (1 - row) * near, near)], a_near, row_peer)]
-    for step in range(columns - 1):
-        source = sums.at[pl.ds(b_base + far[step] * narrow, narrow)]
-        copies.append(push(source, b_far.at[step], far_peers[step]))
-    build_some(0, half)
+    build_some(0, half + part + near)
+    inbox[me] = parcels[me]
     for copy in copies:
         copy.wait()
     a_mine = a_base + row * near
     b_mine = b_base + column * narrow
-    sums[pl.ds(a_mine, near)] = sums[pl.ds(a_mine, near)] + a_near[...]
-    total = sums[pl.ds(b_mine, narrow)]
-    for step in range(columns - 1):
-        total = total + b_far[step]
-    sums[pl.ds(b_mine, narrow)] = total
-
-    copies = [push(sums.at[pl.ds(b_mine + (1 - row) * one, one)], b_near, row_peer)]
-    for step in range(columns - 1):
-        source = sums.at[pl.ds(a_mine + far[step] * one, one)]
-        copies.append(push(source, a_far.at[step], far_peers[step]))
-    build_some(half, half + part + near)
-    for copy in copies:
-        copy.wait()
-    a_one, b_one = a_mine + column * one, b_mine + row * one
-    a_two, b_two = pl.ds(a_one, one), pl.ds(b_one, one)
-    taps[b_two] = sums[b_two] + b_near[...]
-    total = sums[a_two]
-    for step in range(columns - 1):
-        total = total + a_far[step]
-    taps[a_two] = total
+    a_one, b_one = a_mine + column, b_mine + row
+    a_two, b_two = pl.ds(a_one, 1), pl.ds(b_one, 1)
+    chosen = [inbox[owners_ref[batch]].astype(jnp.float32) for batch in range(batch_count)]
+    for at, skip in ((a_one, 0), (b_one, tmpl_count)):
+        taps[at] = jnp.concatenate(
+            [held[skip : skip + tmpl_count] for held in chosen], axis=0
+        ).astype(jnp.bfloat16)
 
     copies = [push(taps.at[b_two], taps.at[b_two], row_peer)]
     for peer in far_peers:
@@ -314,17 +293,29 @@
     copies = [push(taps.at[a_all], taps.at[a_all], row_peer)]
     for peer in far_peers:
         copies.append(push(taps.at[b_all], taps.at[b_all], peer))
+    early = [push(taps.at[held], taps.at[held], core_peer) for held in (a_all, b_all)]
     running = score_some(a_mine, near, running)
     running = score_some(b_mine, narrow, running)
+    for copy in early:
+        copy.wait()
+    twin = (1 - core) * half
+    running = score_some(twin + row * near, near, running)
+    running = score_some(twin + part + column * narrow, narrow, running)
     for copy in copies:
         copy.wait()
 
-    copies = [push(taps.at[mine], taps.at[mine], core_peer)]
-    running = score_some(a_base + (1 - row) * near, near, running)
-    for step in range(columns - 1):
-        running = score_some(b_base + far[step] * narrow, narrow, running)
-    copies[0].wait()
-    running = score_some((1 - core) * half, half, running)
+    a_rest = (1 - row) * near
+    rest = [(a_rest, near)] + [(part + other * narrow, narrow) for other in far]
+    late = []
+    for first, count in rest:
+        held = pl.ds(base + first, count)
+        late.append(push(taps.at[held], taps.at[held], core_peer))
+    for first, count in rest:
+        running = score_some(base + first, count, running)
+    for copy in late:
+        copy.wait()
+    for first, count in rest:
+        running = score_some(twin + first, count, running)
 
     kept = tmpl_count // 2
     for which in range(2):
@@ -363,9 +354,8 @@
     lanes = round_up(comp_count * depth, LANE)
     width = round_up(stretch + MAXM + depth, LANE)
     columns = blocks // 4
-    part = local_sta // 4
     tile = (row_count, lanes)
-    count = 4 + 4 * columns
+    count = blocks + 2 + 2 * columns + 2 + columns
     kept = (row_count // 2, stretch)
     phased = (PHASES * row_count // 2, LANE)
     anywhere = pl.BlockSpec(memory_space=pl.ANY)
@@ -380,12 +370,8 @@
             pltpu.VMEM(data.shape, data.dtype),
             pltpu.VMEM(moveouts.shape, moveouts.dtype),
             pltpu.VMEM((local_sta,) + tile, jnp.bfloat16),
-            pltpu.VMEM((local_sta,) + tile, jnp.bfloat16),
-            pltpu.VMEM((local_sta // 2,) + tile, jnp.bfloat16),
-            pltpu.VMEM((part // 2,) + tile, jnp.bfloat16),
-            pltpu.VMEM((columns - 1, part // 2 // columns) + tile, jnp.bfloat16),
-            pltpu.VMEM((columns - 1, part // columns) + tile, jnp.bfloat16),
-            pltpu.VMEM((part // 2 // columns,) + tile, jnp.bfloat16),
+            pltpu.VMEM((blocks,) + tile, jnp.bfloat16),
+            pltpu.VMEM((blocks,) + tile, jnp.bfloat16),
             pltpu.VMEM((comp_count, local_sta, width - stretch), jnp.bfloat16),
             pltpu.VMEM((comp_count * local_sta, 2 * PHASES, 2 * LANE), jnp.float32),
             pltpu.VMEM((PHASES, local_sta, LANE), jnp.float32),
@@ -471,8 +457,9 @@
         lax.axis_size("sta") == 2
         and blocks % 4 == 0
         and blocks > 4
-        and local_sta % (2 * blocks) == 0
-        and row_count % SUB == 0
+        and local_sta == 2 * blocks
+        and row_count == SUB
+        and owners.shape[0] == 2
         and bank.shape[1] % 2 == 0
         and stretch % LANE == 0
         and stretch >= round_up(reach, LANE)

time: 39 us -> 35.5 us (0.910)
  Pallas kernels: 37.5 us -> 34 us
    pallas_call x1, Pallas kernels: 37.5 us -> 34 us  [network(): pl.pallas_call(functools.partial(network_kernel, blocks), out_shape=jax.S...]
where the time goes in v4:
time: 35.5 us; the launch traced here: 35.3 us
  Pallas kernels  34 us (96%)
  local copies, waits for them, and re-layouts  1.31 us (4%)
    pallas_call x1, Pallas kernels, network(): pl.pallas_call(functools.partial(network_kernel, blocks), out_shape=jax.S...  34 us
    reshape x1, local copies, waits for them, and re-layouts, shards(): return kept.reshape(batch_count, tmpl_count // 2, stretch)  1.31 us

profile of v4, /device:TPU:0, one launch (start us, length us, event | category | flops | bytes accessed | tf_op | source)
XLA Modules:
  0.0 35.3 jit_solution(18390751109177371472)
XLA Ops:
  0.0 34.0 %shard_map.46 = f32[8,384]{1,0:T(8,128)} custom-call(bf16[8,3,32,150]{3,2,1,0:T(8,128)(2,1)} %bitcast.5, s32[2]{0:T(128)} %owners_ref.1, bf16[3,32,384]{2,1,0:T(8,128)(2,1)} %bitcast.6, s32[16,32]{1,0:T(8,128)} %bitcast.7), custom_call_target="tpu_custom_call" | custom-call | tf_op jit(solution)/shard_map/pallas_call | solution.py:363
  34.0 1.3 %reshape.7 = f32[2,4,384]{2,1,0:T(4,128)} reshape(f32[8,384]{1,0:T(8,128)} %shard_map.46) | data formatting | bytes 24576 | tf_op jit(solution)/shard_map/reshape | solution.py:488

commit v5 on v4

--- a/solution.py
+++ b/solution.py
@@ -134,7 +134,9 @@
     row_peer = place(column, 1 - row, core)
     far = [(column + step) % columns for step in range(1, columns)]
     far_peers = [place(other, row, core) for other in far]
-    others = [(me + step) % blocks for step in range(1, blocks)]
+    steps = sorted(range(1, blocks), key=lambda step: abs(2 * step - blocks))
+    others = [(me + step) % blocks for step in steps]
+    before = {"tm": (me + blocks - 1) % blocks}
     sta_peer = {"sta": 1 - side}
 
     barrier = pltpu.get_barrier_semaphore()
@@ -234,11 +236,10 @@
 
     base = core * half
     a_base, b_base = base, base + part
-    mine = pl.ds(base, half)
-
+
+    loads[1].wait()
+    edge_copy = push(data_ref.at[:, :, pl.ds(0, edge_in.shape[2])], edge_in, before)
     copies = [push(parcels.at[other], inbox.at[me], {"tm": other}) for other in others]
-    loads[1].wait()
-    edge_copy = push(data_ref.at[:, :, pl.ds(0, edge_in.shape[2])], edge_in, {"tm": others[-1]})
     loads[2].wait()
     delays = moveouts_ref[...]
     for station in range(local_sta):
@@ -267,33 +268,40 @@
     rows[...] = jnp.swapaxes(jnp.stack(phased + phased, axis=0), 0, 1)
     for phase, energy in enumerate(phase_energies(squares, span)):
         power[phase] = (1.0 / jnp.sqrt(energy * scale + eps))[:, :LANE]
-    build_some(0, half + part + near)
+    build_some(0, half + part)
     inbox[me] = parcels[me]
     for copy in copies:
         copy.wait()
     a_mine = a_base + row * near
     b_mine = b_base + column * narrow
     a_one, b_one = a_mine + column, b_mine + row
-    a_two, b_two = pl.ds(a_one, 1), pl.ds(b_one, 1)
     chosen = [inbox[owners_ref[batch]].astype(jnp.float32) for batch in range(batch_count)]
     for at, skip in ((a_one, 0), (b_one, tmpl_count)):
         taps[at] = jnp.concatenate(
             [held[skip : skip + tmpl_count] for held in chosen], axis=0
         ).astype(jnp.bfloat16)
 
-    copies = [push(taps.at[b_two], taps.at[b_two], row_peer)]
-    for peer in far_peers:
-        copies.append(push(taps.at[a_two], taps.at[a_two], peer))
-    build_some(half + part + near, local_sta)
+    def share(first, peer, count=1):
+        held = taps.at[pl.ds(first, count)]
+        return push(held, held, peer)
+
+    b_row = share(b_one, row_peer)
+    b_far = [share(b_one, peer) for peer in far_peers]
+    a_far = [share(a_one, peer) for peer in far_peers]
+    a_row = [share(a_one, row_peer)]
+    early = [share(b_one, core_peer), share(a_one, core_peer)]
+    build_some(half + part, local_sta - near)
+    b_row.wait()
+    b_other = b_mine + 1 - row
+    b_far += [share(b_other, peer) for peer in far_peers]
+    early.append(share(b_other, core_peer))
+    build_some(local_sta - near, local_sta)
+    for step in range(columns - 1):
+        a_far[step].wait()
+        arrived = a_mine + (column + columns - 1 - step) % columns
+        a_row.append(share(arrived, row_peer))
+        early.append(share(arrived, core_peer))
     running = (jnp.zeros((row_count, LANE), jnp.float32),) * PHASES
-    for copy in copies:
-        copy.wait()
-
-    a_all, b_all = pl.ds(a_mine, near), pl.ds(b_mine, narrow)
-    copies = [push(taps.at[a_all], taps.at[a_all], row_peer)]
-    for peer in far_peers:
-        copies.append(push(taps.at[b_all], taps.at[b_all], peer))
-    early = [push(taps.at[held], taps.at[held], core_peer) for held in (a_all, b_all)]
     running = score_some(a_mine, near, running)
     running = score_some(b_mine, narrow, running)
     for copy in early:
@@ -301,15 +309,14 @@
     twin = (1 - core) * half
     running = score_some(twin + row * near, near, running)
     running = score_some(twin + part + column * narrow, narrow, running)
-    for copy in copies:
+    for copy in a_row + b_far:
         copy.wait()
 
     a_rest = (1 - row) * near
     rest = [(a_rest, near)] + [(part + other * narrow, narrow) for other in far]
     late = []
     for first, count in rest:
-        held = pl.ds(base + first, count)
-        late.append(push(taps.at[held], taps.at[held], core_peer))
+        late.append(share(base + first, core_peer, count))
     for first, count in rest:
         running = score_some(base + first, count, running)
     for copy in late:
@@ -342,7 +349,8 @@
             precision=lax.Precision.HIGHEST,
             preferred_element_type=jnp.float32,
         )
-    out_ref[...] = result
+    for batch in range(batch_count):
+        out_ref[batch] = result[batch * kept : (batch + 1) * kept]
 
 
 def network(slot, owners, data, moveouts, blocks):
@@ -355,8 +363,8 @@
     width = round_up(stretch + MAXM + depth, LANE)
     columns = blocks // 4
     tile = (row_count, lanes)
-    count = blocks + 2 + 2 * columns + 2 + columns
-    kept = (row_count // 2, stretch)
+    count = blocks + 8 + 6 * columns
+    kept = (batch_count, tmpl_count // 2, stretch)
     phased = (PHASES * row_count // 2, LANE)
     anywhere = pl.BlockSpec(memory_space=pl.ANY)
     in_vmem = pl.BlockSpec(memory_space=pltpu.VMEM)
@@ -478,14 +486,13 @@
     row_count = batch_count * tmpl_count
     blocks = lax.axis_size("tm")
     if fits(data, bank, owners):
-        kept = network(
+        return network(
             jnp.transpose(bank[0], (0, 2, 1, 3)),
             owners,
             jnp.transpose(data, (1, 0, 2)),
             moveouts.reshape(row_count, local_sta),
             blocks,
         )
-        return kept.reshape(batch_count, tmpl_count // 2, stretch)
 
     edge = span - 1 + MAXM
     width = round_up(stretch + MAXM + round_up(span, SUB), LANE)

time: 35.5 us -> 34.1 us (0.961)
  Pallas kernels: 34 us -> 32.6 us
    pallas_call x1, Pallas kernels: 34 us -> 32.6 us  [network(): pl.pallas_call(functools.partial(network_kernel, blocks), out_shape=jax.S...]
    reshape x1 -> x0, local copies, waits for them, and re-layouts: 1.31 us -> none  [shards(): return kept.reshape(batch_count, tmpl_count // 2, stretch)]
    unnamed x0 -> x1, local copies, waits for them, and re-layouts: none -> 1.31 us
where the time goes in v5:
time: 34.1 us; the launch traced here: 33.9 us
  Pallas kernels  32.6 us (96%)
  local copies, waits for them, and re-layouts  1.31 us (4%)
    pallas_call x1, Pallas kernels, network(): pl.pallas_call(functools.partial(network_kernel, blocks), out_shape=jax.S...  32.6 us
    unnamed x1, local copies, waits for them, and re-layouts  1.31 us

profile of v5, /device:TPU:0, one launch (start us, length us, event | category | flops | bytes accessed | tf_op | source)
XLA Modules:
  0.0 33.9 jit_solution(4011475557834256230)
XLA Ops:
  0.0 32.6 %shard_map.46 = f32[2,4,384]{2,1,0:T(4,128)} custom-call(bf16[8,3,32,150]{3,2,1,0:T(8,128)(2,1)} %bitcast.5, s32[2]{0:T(128)} %owners_ref.1, bf16[3,32,384]{2,1,0:T(8,128)(2,1)} %bitcast.6, s32[16,32]{1,0:T(8,128)} %bitcast.7), custom_call_target="tpu_custom_call" | custom-call | tf_op jit(solution)/shard_map/pallas_call | solution.py:371
  32.6 1.3 %copy.6 = f32[2,4,384]{2,1,0:T(4,128)} copy(f32[2,4,384]{2,1,0:T(4,128)} %shard_map.46) | data formatting | bytes 24576

commit v6 on v5

--- a/solution.py
+++ b/solution.py
@@ -227,11 +227,11 @@
         return tuple(held + score for held, score in zip(running, scores))
 
     def build_some(first, last):
-        lax.fori_loop(first, last, build, 0, unroll=2)
+        lax.fori_loop(first, last, build, 0, unroll=4)
 
     def score_some(first, count, running):
         return lax.fori_loop(
-            0, count, lambda i, held: score(first + i, held), running, unroll=min(count, 2)
+            0, count, lambda i, held: score(first + i, held), running, unroll=min(count, 4)
         )
 
     base = core * half

time: 34.1 us -> 33 us (0.968)
  Pallas kernels: 32.6 us -> 31.5 us
    pallas_call x1, Pallas kernels: 32.6 us -> 31.5 us  [network(): pl.pallas_call(functools.partial(network_kernel, blocks), out_shape=jax.S...]
where the time goes in v6:
time: 33 us; the launch traced here: 32.8 us
  Pallas kernels  31.5 us (95%)
  local copies, waits for them, and re-layouts  1.31 us (4%)
    pallas_call x1, Pallas kernels, network(): pl.pallas_call(functools.partial(network_kernel, blocks), out_shape=jax.S...  31.5 us
    unnamed x1, local copies, waits for them, and re-layouts  1.31 us

profile of v6, /device:TPU:0, one launch (start us, length us, event | category | flops | bytes accessed | tf_op | source)
XLA Modules:
  0.0 32.8 jit_solution(542141283739735310)
XLA Ops:
  0.0 31.5 %shard_map.46 = f32[2,4,384]{2,1,0:T(4,128)} custom-call(bf16[8,3,32,150]{3,2,1,0:T(8,128)(2,1)} %bitcast.5, s32[2]{0:T(128)} %owners_ref.1, bf16[3,32,384]{2,1,0:T(8,128)(2,1)} %bitcast.6, s32[16,32]{1,0:T(8,128)} %bitcast.7), custom_call_target="tpu_custom_call" | custom-call | tf_op jit(solution)/shard_map/pallas_call | solution.py:371
  31.5 1.3 %copy.6 = f32[2,4,384]{2,1,0:T(4,128)} copy(f32[2,4,384]{2,1,0:T(4,128)} %shard_map.46) | data formatting | bytes 24576
